TPU v7x, 32 devices: a whole 2x2x4 slice. The times are simulated.
32 devices in a mesh: rep: 8 (over z, y), fsdp: 4 (over x, core).
Axes of the slice: x: 2, y: 2, z: 4, core: 2. Of those that a mesh axis runs over, the one named last changes fastest.
Arguments:
- token_ids: int32 [8, 1024], P('rep', 'fsdp'), may hold values from 0 to 128004, as said below
- hidden: bfloat16 [8, 1024, 4096], P('rep', 'fsdp'), may hold values from -600 to 600
- norm_gain: float32 [8, 4096], P('rep'), may hold values from 0.5 to 1.5
- key_weight: bfloat16 [8, 4096, 512], P('rep', 'fsdp'), may hold values from -0.09375 to 0.09375
- key_cot: bfloat16 [8, 1024, 512], P('rep', 'fsdp'), may hold values from -0.119628906 to 0.119628906
- frag_base: float32 [4096, 512], P('fsdp'), may hold values from -3 to 3
- frag_local: bfloat16 [8, 4096, 512], P('rep', 'fsdp'), may hold values from -16 to 16
- momentum: bfloat16 [4096, 512], P('fsdp'), may hold values from -1.796875 to 1.796875
Outputs:
- keys: bfloat16 [8, 1024, 512], P('rep', 'fsdp')
- weight_grad: bfloat16 [8, 4096, 512], P('rep', 'fsdp')
- gain_grad: float32 [8, 4096], P('rep')
- new_params: float32 [4096, 512], P('fsdp')
- new_momentum: bfloat16 [4096, 512], P('fsdp')
Inputs may be any that keep to these rules, and one draw needn't show every extreme that they name: `token_ids`: each aligned sequence of 64 ids holds between 16 and 63 ordinary ids, each below 128000, followed by the padding id 128004 up to its end.
All inputs are finite; a program needn't handle non-finite values.
Results may differ from a plain program's by a relative error of at most 0.009.
Values may be sent and summed in bfloat16 or wider, within the bound.
A program may use at most 128 MiB of HBM per device.

v0:
```python
import jax
import jax.numpy as jnp
from jax import lax
from jax.sharding import PartitionSpec as P

LEN = 64


pad_token = 128004
norm_eps = 1e-05
nesterov_mu = 0.9
outer_rate = 0.7


def loss_weights(token_ids):
    grouped = token_ids.reshape(token_ids.shape[0], -1, LEN)
    is_live = (grouped != pad_token).astype(jnp.float32)
    live_count = jnp.sum(is_live, -1, keepdims=True)
    return (LEN * is_live / live_count).reshape(token_ids.shape[0], -1)


def inner_step(token_ids, hidden, norm_gain, key_weight, key_cot):
    x_float = hidden[0].astype(jnp.float32)
    inv_rms = lax.rsqrt(jnp.mean(x_float * x_float, -1, keepdims=True) + norm_eps)
    scaled = x_float * inv_rms
    normed = (scaled * norm_gain[0]).astype(jnp.bfloat16)
    loss_weight = loss_weights(token_ids)[0]
    weighted = (loss_weight[:, None] * key_cot[0].astype(jnp.float32)).astype(jnp.bfloat16)
    w_rows = lax.all_gather(key_weight, "fsdp", axis=1, tiled=True)[0]
    h_cols = normed
    keys_acc = jnp.dot(h_cols, w_rows, preferred_element_type=jnp.float32)
    grad_cols = lax.dot_general(
        weighted, w_rows, (((1,), (1,)), ((), ())), preferred_element_type=jnp.float32
    )
    gain_acc = jnp.sum(grad_cols * scaled, 0)
    keys_acc, gain_part = (keys_acc, gain_acc)
    gain_grad = lax.psum(gain_part, "fsdp")
    h_cols = normed
    weight_grad = lax.psum_scatter(
        lax.dot_general(
            h_cols, weighted, (((0,), (0,)), ((), ())), preferred_element_type=jnp.float32
        ).astype(jnp.bfloat16),
        "fsdp",
        scatter_dimension=0,
        tiled=True,
    )
    return (keys_acc.astype(jnp.bfloat16)[None], weight_grad[None], gain_grad[None])


def outer_step(frag_base, frag_local, momentum):
    replicas = lax.axis_size("rep")
    pseudo_grad = (frag_base - frag_local[0].astype(jnp.float32)).astype(jnp.bfloat16)
    grads_all = lax.all_gather(pseudo_grad[None], "rep", axis=0, tiled=True)
    outer_grad = jnp.sum(grads_all.astype(jnp.float32), 0) / replicas
    momentum_next = nesterov_mu * momentum.astype(jnp.float32) + outer_grad
    new_params = frag_base - outer_rate * (nesterov_mu * momentum_next + outer_grad)
    return (new_params, momentum_next.astype(jnp.bfloat16))


def body(token_ids, hidden, norm_gain, key_weight, key_cot, frag_base, frag_local, momentum):
    keys, weight_grad, gain_grad = inner_step(token_ids, hidden, norm_gain, key_weight, key_cot)
    new_params, new_momentum = outer_step(frag_base, frag_local, momentum)
    return (keys, weight_grad, gain_grad, new_params, new_momentum)


def solution(mesh):
    return jax.shard_map(
        body,
        mesh=mesh,
        in_specs=(
            P("rep", "fsdp"),
            P("rep", "fsdp", None),
            P("rep", None),
            P("rep", "fsdp", None),
            P("rep", "fsdp", None),
            P("fsdp", None),
            P("rep", "fsdp", None),
            P("fsdp", None),
        ),
        out_specs=(
            P("rep", "fsdp", None),
            P("rep", "fsdp", None),
            P("rep", None),
            P("fsdp", None),
            P("fsdp", None),
        ),
        check_vma=False,
    )
```

profile of v0, /device:TPU:0, one launch (start us, length us, event | category | flops | bytes accessed | tf_op | source)
XLA Modules:
  0.0 226.8 jit_solution(5479672775614525031)
XLA Ops:
  7.2 0.0 all-gather.4.cloned.1.call-start
  7.2 0.7 all-gather.4.cloned.1.call-update
  7.9 0.0 copy-start.3
  7.9 0.0 all-gather.6.cloned.1.call-start
  8.0 3.3 %fusion.9 = bf16[1024,512]{1,0:T(8,128)(2,1)} fusion(f32[1024,512]{1,0:T(8,128)} %param.13, bf16[1,1024,512]{2,1,0:T(8,128)(2,1)} %param.14), kind=kLoop, calls=%fused_computation.15 | loop fusion | flops 1572864 | bytes 4194304 | tf_op jit(solution)/shard_map/convert_element_type | solution.py:52
  11.3 0.0 all-gather.6.cloned.1.call-update
  11.3 0.0 reduce-scatter.2.cloned.1.call-start
  11.4 0.1 reshape.117
  11.5 0.1 reduce_sum.37
  11.6 0.1 broadcast_reduce_fusion
  11.7 0.1 div.31
  11.8 0.5 fusion.2
  12.3 0.0 copy-done.4
  12.3 0.0 copy-done.5
  12.3 3.4 %convolution_convert_fusion = bf16[4096,512]{1,0:T(8,128)(2,1)} fusion(bf16[1,256,4096]{2,1,0:T(8,128)(2,1)S(1)} %copy-done.1, f32[4096]{0:T(1024)S(1)} %bitcast.46, f32[256]{0:T(256)S(1)} %add_rsqrt_fusion, bf16[1,256,512]{2,1,0:T(8,128)(2,1)S(1)} %copy-done.4, f32[256]{0:T(256)S(1)} %div.32), kind=kOutput, calls=%fused_computation.1 | convolution fusion | flops 1080426496 | bytes 6572032 | tf_op jit(solution)/shard_map/dot_general | solution.py:40
  15.8 0.0 reduce-scatter.2.cloned.1.call-update
  15.8 31.0 %all-gather.4.cloned.1.call-done = bf16[1,4096,512]{2,1,0:T(8,128)(2,1)} async-done(((bf16[1,1024,512]{2,1,0:T(8,128)(2,1)}), bf16[1,4096,512]{2,1,0:T(8,128)(2,1)}) %all-gather.4.cloned.1.call-update) | async-done | bytes 4194320 | tf_op jit(solution)/shard_map/all_gather | solution.py:29
  46.8 3.5 %fusion.11 = f32[4096]{0:T(1024)S(1)} fusion(f32[256]{0:T(256)S(1)} %add_rsqrt_fusion, bf16[1,256,4096]{2,1,0:T(8,128)(2,1)S(1)} %copy-done.1, bf16[1,4096,512]{2,1,0:T(8,128)(2,1)} %all-gather.4.cloned.1.call-done, bf16[1,256,512]{2,1,0:T(8,128)(2,1)S(1)} %copy-done.4, f32[256]{0:T(256)S(1)} %div.32), kind=kOutput, calls=%fused_computation.19 | convolution fusion | flops 1078325248 | bytes 6572032 | tf_op jit(solution)/shard_map/dot_general | solution.py:32
  50.3 10.8 %psum.7 = f32[1,4096]{1,0:T(1,128)} all-reduce(f32[1,4096]{1,0:T(1,128)S(1)} %bitcast.43), channel_id=1, replica_groups=mesh['rep'=8,'fsdp'=4] {'fsdp'}, use_global_device_ids=true, to_apply=%region_4.0 | all-reduce | flops 4096 | bytes 32768 | tf_op jit(solution)/shard_map/psum | solution.py:37
  61.1 4.2 %fusion.17 = bf16[1,256,512]{2,1,0:T(8,128)(2,1)} fusion(bf16[1,4096,512]{2,1,0:T(8,128)(2,1)} %all-gather.4.cloned.1.call-done, bf16[1,256,4096]{2,1,0:T(8,128)(2,1)S(1)} %copy-done.1, f32[4096]{0:T(1024)S(1)} %bitcast.47, f32[256]{0:T(256)S(1)} %add_rsqrt_fusion), kind=kOutput, calls=%fused_computation.21 | convolution fusion | flops 1078067200 | bytes 6571008 | tf_op jit(solution)/shard_map/dot_general | solution.py:31
  65.3 109.2 %all-gather.6.cloned.1.call-done = bf16[8192,512]{1,0:T(8,128)(2,1)} async-done(((bf16[1024,512]{1,0:T(8,128)(2,1)}), bf16[8192,512]{1,0:T(8,128)(2,1)}) %all-gather.6.cloned.1.call-update) | async-done | bytes 8388624 | tf_op jit(solution)/shard_map/all_gather | solution.py:53
  174.5 4.9 %convert_reduce_fusion = f32[1024,512]{1,0:T(8,128)S(1)} fusion(bf16[8,1024,512]{2,1,0:T(8,128)(2,1)} %bitcast.42), kind=kLoop, calls=%fused_computation | loop fusion | flops 7864320 | bytes 10485760 | tf_op jit(solution)/shard_map/reduce_sum | solution.py:54
  179.4 2.4 %fusion.10 = (bf16[1024,512]{1,0:T(8,128)(2,1)}, f32[1024,512]{1,0:T(8,128)}) fusion(bf16[1024,512]{1,0:T(8,128)(2,1)S(1)} %copy-done.2, f32[1024,512]{1,0:T(8,128)S(1)} %convert_reduce_fusion, f32[1024,512]{1,0:T(8,128)S(1)} %copy-done), kind=kLoop, calls=%fused_computation.18 | loop fusion | flops 4718592 | bytes 8388608 | tf_op jit(solution)/shard_map/convert_element_type | solution.py:57
  181.8 38.5 %reduce-scatter.2.cloned.1.call-done = bf16[1024,512]{1,0:T(8,128)(2,1)} async-done(((bf16[4096,512]{1,0:T(8,128)(2,1)}), bf16[1024,512]{1,0:T(8,128)(2,1)}) %reduce-scatter.2.cloned.1.call-update) | async-done | bytes 1048592 | tf_op jit(solution)/shard_map/reduce_scatter | solution.py:39
  (12 shorter events, 0.1 us)
Async XLA Ops:
  7.2 39.6 %all-gather.4.cloned.1.call-start = ((), (), s32[]{:S(2)}) async-start(), calls=%async_computation.1 | async-start | bytes 5242880 | tf_op jit(solution)/shard_map/all_gather | solution.py:29
  7.9 3.5 %copy-start.3 = (s32[1,256]{1,0:T(1,128)S(1)}, s32[1,256]{1,0:T(1,128)}, u32[]{:S(2)}) copy-start(s32[1,256]{1,0:T(1,128)} %param.8) | copy-start | bytes 3076
  7.9 3.9 %copy-start.1 = (bf16[1,256,4096]{2,1,0:T(8,128)(2,1)S(1)}, bf16[1,256,4096]{2,1,0:T(8,128)(2,1)}, u32[]{:S(2)}) copy-start(bf16[1,256,4096]{2,1,0:T(8,128)(2,1)} %param.9) | copy-start | bytes 6291460
  7.9 166.5 %all-gather.6.cloned.1.call-start = ((), (), s32[]{:S(2)}) async-start(), calls=%async_computation.3 | async-start | bytes 9437184 | tf_op jit(solution)/shard_map/all_gather | solution.py:53
  11.3 1.0 copy-start.4
  11.3 1.0 copy-start.5
  11.3 209.0 %reduce-scatter.2.cloned.1.call-start = ((), (), s32[]{:S(2)}) async-start(), calls=%async_computation.2 | async-start | bytes 5242880 | tf_op jit(solution)/shard_map/reduce_scatter | solution.py:39
  174.5 4.9 %copy-start = (f32[1024,512]{1,0:T(8,128)S(1)}, f32[1024,512]{1,0:T(8,128)}, u32[]{:S(2)}) copy-start(f32[1024,512]{1,0:T(8,128)} %param.13) | copy-start | bytes 6291460
  174.5 5.0 %copy-start.2 = (bf16[1024,512]{1,0:T(8,128)(2,1)S(1)}, bf16[1024,512]{1,0:T(8,128)(2,1)}, u32[]{:S(2)}) copy-start(bf16[1024,512]{1,0:T(8,128)(2,1)} %param.15) | copy-start | bytes 3145732
Sparse Core Ops, SparseCore 0:
  9.6 37.1 all-gather.3
  49.5 124.9 all-gather.5
  177.6 42.6 reduce-scatter.1
where the time goes:
time: 227 us
  waiting for transfers between devices  179 us (79%)
  between operations  13.8 us (6%)
  other arithmetic  11.3 us (5%)
  matrix products  11.1 us (5%)
  blocking collectives  10.8 us (5%)
    all_gather x1, waiting for transfers between devices, outer_step(): grads_all = lax.all_gather(pseudo_grad[None], 'rep', axis=0, tiled=True)  109 us
    reduce_scatter x1, waiting for transfers between devices, inner_step(): lax.psum_scatter(lax.dot_general(h_cols, weighted, (((0,), (0,)), ((), ()...  38.5 us
    all_gather x1, waiting for transfers between devices, inner_step(): w_rows = lax.all_gather(key_weight, 'fsdp', axis=1, tiled=True)[0]  31 us
    psum x1, blocking collectives, inner_step(): gain_grad = lax.psum(gain_part, 'fsdp')  10.8 us
    reduce_sum x1, other arithmetic, outer_step(): outer_grad = jnp.sum(grads_all.astype(jnp.float32), 0) / replicas  4.93 us
  transfers between devices with their start and end apart: 3, of which 3 were waited for; matrix products, arithmetic and copies ran while one was open for 10% of the time, Pallas kernels for 0%

commit v1 on v0

v1 whole, which is shorter than its diff:
```python
import functools

import jax
import jax.numpy as jnp
from jax import lax
from jax.experimental import pallas as pl
from jax.experimental.pallas import tpu as pltpu
from jax.sharding import PartitionSpec as P

LEN = 64
LANES = 128
CORES = 2
PAIR = 2
CHUNKS = 4

pad_token = 128004
norm_eps = 1e-05
nesterov_mu = 0.9
outer_rate = 0.7

MESH = pl.DeviceIdType.MESH


class Counter:
    def __init__(self):
        self.n = 0

    def take(self, count=1):
        first = self.n
        self.n += count
        return first


def semaphore_plan(nf, nr):
    chips, outer = nf // CORES, nr // PAIR
    c = Counter()
    plan = {
        "w": c.take(),
        "sib": c.take(),
        "wt_sib": c.take(),
        "wt": c.take(chips),
        "wt_fwd": c.take(chips),
        "nrm": c.take(chips * CHUNKS),
        "fwd": c.take(chips * CHUNKS),
        "kp": c.take(chips * CHUNKS),
        "gain": c.take(nf),
        "y": c.take(2),
        "z": c.take(2 * outer),
        "zag": c.take(2 * outer),
        "yag": c.take(2),
    }
    return plan, c.n


def transposed_dot(a, b):
    return lax.dot_general(a, b, (((0,), (0,)), ((), ())), preferred_element_type=jnp.float32)


def kernel(
    nf, nr, plan,
    ids_h, hid_h, gain_h, w_h, cot_h, base_h, loc_h,
    keys_h, wgrad_h, ggrad_h, outer_h,
    ids, hid, gain, wch, cot, base, loc,
    nrm, rn, sn, fn, wt, wt_s, wt_p, wt_f, pk, kp, kacc, kout,
    grad, wout, gg, gout,
    ps, yr, ys, zr, og,
    ss, rs, ls,
):
    tok = hid.shape[0]
    dn = base.shape[0]
    chips, outer = nf // CORES, nr // PAIR
    zrows = dn // outer
    ct = tok // CHUNKS
    f = lax.axis_index("fsdp")
    r = lax.axis_index("rep")
    x, c = lax.div(f, CORES), lax.rem(f, CORES)
    sib = f + 1 - 2 * c
    z, h = lax.div(r, PAIR), lax.rem(r, PAIR)
    partner = r + 1 - 2 * h

    def chip_at(j):
        return lax.rem(x + j, chips)

    def z_at(j):
        return lax.rem(z + j, outer)

    def local(i, src, dst):
        copy = pltpu.make_async_copy(src, dst, ls.at[i])
        copy.start()
        return copy

    l_cot = local(0, cot_h.at[0], cot)
    l_ids = local(1, ids_h, ids)
    l_gain = local(2, gain_h, gain)
    l_hid = local(3, hid_h.at[0], hid)
    l_w = local(4, w_h.at[0], wch.at[c])
    l_base = local(5, base_h, base)
    l_loc = local(6, loc_h.at[0], loc)

    barrier = pltpu.get_barrier_semaphore()
    greeted = 0
    for o in range(1, nf):
        pl.semaphore_signal(barrier, inc=1, device_id={"fsdp": lax.rem(f + o, nf)}, device_id_type=MESH)
        greeted += 1
    pl.semaphore_signal(barrier, inc=1, device_id={"rep": partner}, device_id_type=MESH)
    greeted += 1
    for o in range(1, outer):
        pl.semaphore_signal(barrier, inc=1, device_id={"rep": z_at(o) * PAIR + h}, device_id_type=MESH)
        greeted += 1

    sent = []

    def copy_of(src, dst, sid, rid, dev):
        return pltpu.make_async_remote_copy(
            src_ref=src, dst_ref=dst, send_sem=ss.at[sid], recv_sem=rs.at[rid],
            device_id=dev, device_id_type=MESH,
        )

    def send(src, dst, sid, rid, dev):
        copy = copy_of(src, dst, sid, rid, dev)
        copy.start()
        sent.append(copy)

    def arrived(dst, rid):
        copy_of(dst, dst, rid, rid, {"fsdp": sib}).wait_recv()

    l_ids.wait()
    row = lax.broadcasted_iota(jnp.int32, (tok, tok), 0)
    col = lax.broadcasted_iota(jnp.int32, (tok, tok), 1)
    live = jnp.where(ids[...] != pad_token, 1.0, 0.0).astype(jnp.float32)
    live = jnp.broadcast_to(live, (tok, tok))
    count = jnp.sum(jnp.where(lax.div(row, LEN) == lax.div(col, LEN), live, 0.0), -1, keepdims=True)
    own = jnp.sum(jnp.where(row == col, live, 0.0), -1, keepdims=True)
    loss_weight = LEN * own / count
    l_cot.wait()
    wt[...] = (loss_weight * cot[...].astype(jnp.float32)).astype(jnp.bfloat16)

    pl.semaphore_wait(barrier, greeted)

    def peer(j):
        return {"fsdp": chip_at(j) * CORES + c}

    for j in range(1, chips):
        send(wt, wt_p.at[chips - j], plan["wt"] + j, plan["wt"] + chips - j, peer(j))
    send(wt, wt_s, plan["wt_sib"], plan["wt_sib"], {"fsdp": sib})
    send(w_h.at[0], wch.at[c], plan["w"], plan["w"], {"fsdp": sib})

    l_gain.wait()
    l_hid.wait()
    sub = 16

    def norm_rows(i, carry):
        rows = pl.ds(pl.multiple_of(i * sub, sub), sub)
        v = hid[rows, :].astype(jnp.float32)
        inv = lax.rsqrt(jnp.mean(v * v, -1, keepdims=True) + norm_eps)
        for d in range(nf):
            part = hid[rows, d * dn:(d + 1) * dn].astype(jnp.float32)
            nrm[d, rows, :] = (part * inv * gain[:, d * dn:(d + 1) * dn]).astype(jnp.bfloat16)
        return carry

    for q in range(CHUNKS):
        lax.fori_loop(q * (ct // sub), (q + 1) * (ct // sub), norm_rows, 0)
        rows = pl.ds(q * ct, ct)
        for j in range(1, chips):
            send(
                nrm.at[pl.ds(chip_at(j) * CORES, CORES), rows, :],
                rn.at[chips - j, :, rows, :],
                plan["nrm"] + j * CHUNKS + q,
                plan["nrm"] + (chips - j) * CHUNKS + q,
                peer(j),
            )
    send(nrm.at[sib], sn, plan["sib"], plan["sib"], {"fsdp": sib})

    l_base.wait()
    l_loc.wait()
    step = 64

    def pseudo_rows(i, carry):
        rows = pl.ds(pl.multiple_of(i * step, step), step)
        for g in range(4):
            cols = slice(g * LANES, (g + 1) * LANES)
            ps[g, rows, :] = (base[rows, cols] - loc[rows, cols].astype(jnp.float32)).astype(jnp.bfloat16)
        return carry

    lax.fori_loop(0, dn // step, pseudo_rows, 0)
    for k in range(2):
        send(ps.at[2 * (1 - h) + k], yr.at[k], plan["y"] + k, plan["y"] + k, {"rep": partner})

    l_w.wait()
    arrived(wch.at[1 - c], plan["w"])
    kacc[...] = jnp.dot(nrm[2 * x], wch[0], preferred_element_type=jnp.float32)
    kacc[...] += jnp.dot(nrm[2 * x + 1], wch[1], preferred_element_type=jnp.float32)

    tile = min(256, dn)

    def grad_tiles(rows_of, tokens_of, first):
        for i in range(dn // tile):
            cut = slice(i * tile, (i + 1) * tile)
            term = transposed_dot(rows_of(cut), tokens_of[...])
            if first:
                grad[cut, :] = term
            else:
                grad[cut, :] += term

    grad_tiles(lambda cut: nrm[f, :, cut], wt, True)
    arrived(wt_s, plan["wt_sib"])
    arrived(sn, plan["sib"])
    grad_tiles(lambda cut: sn[:, cut], wt_s, False)

    for j in range(1, chips):
        arrived(wt_p.at[j], plan["wt"] + j)
        send(wt_p.at[j], wt_f.at[j], plan["wt_fwd"] + j, plan["wt_fwd"] + j, {"fsdp": sib})

    def peer_chunk(q):
        rows = pl.ds(q * ct, ct)
        for j in range(1, chips):
            arrived(rn.at[j, :, rows, :], plan["nrm"] + j * CHUNKS + q)
            send(
                rn.at[j, 1 - c, rows, :], fn.at[j, rows, :],
                plan["fwd"] + j * CHUNKS + q, plan["fwd"] + j * CHUNKS + q, {"fsdp": sib},
            )
            part = jnp.dot(rn[j, 0, rows, :], wch[0], preferred_element_type=jnp.float32)
            part += jnp.dot(rn[j, 1, rows, :], wch[1], preferred_element_type=jnp.float32)
            pk[j, rows, :] = part.astype(jnp.bfloat16)
            send(
                pk.at[j, rows, :], kp.at[chips - j, rows, :],
                plan["kp"] + j * CHUNKS + q, plan["kp"] + (chips - j) * CHUNKS + q, peer(j),
            )

    def pair_sum(k):
        arrived(yr.at[k], plan["y"] + k)
        ys[k] = (ps[2 * h + k].astype(jnp.float32) + yr[k].astype(jnp.float32)).astype(jnp.bfloat16)
        for o in range(1, outer):
            send(
                ys.at[k, pl.ds(pl.multiple_of(z_at(o) * zrows, 16), zrows), :],
                zr.at[k, outer - o],
                plan["z"] + k * outer + o, plan["z"] + k * outer + outer - o,
                {"rep": z_at(o) * PAIR + h},
            )

    mine = pl.ds(pl.multiple_of(z * zrows, 16), zrows)

    def outer_sum(k):
        total = ys[k, mine, :].astype(jnp.float32)
        for o in range(1, outer):
            arrived(zr.at[k, o], plan["z"] + k * outer + o)
            total += zr[k, o].astype(jnp.float32)
        og[2 * h + k, mine, :] = total.astype(jnp.bfloat16)
        for o in range(1, outer):
            send(
                og.at[2 * h + k, mine, :], og.at[2 * h + k, mine, :],
                plan["zag"] + k * outer + o, plan["zag"] + k * outer + outer - o,
                {"rep": z_at(o) * PAIR + h},
            )

    def outer_back(k):
        for o in range(1, outer):
            there = pl.ds(pl.multiple_of(z_at(o) * zrows, 16), zrows)
            arrived(og.at[2 * h + k, there, :], plan["zag"] + k * outer + o)
        send(og.at[2 * h + k], og.at[2 * h + k], plan["yag"] + k, plan["yag"] + k, {"rep": partner})

    peer_chunk(0)
    pair_sum(0)
    peer_chunk(1)
    pair_sum(1)
    outer_sum(0)
    peer_chunk(2)
    outer_sum(1)
    outer_back(0)
    peer_chunk(3)
    outer_back(1)

    for j in range(1, chips):
        grad_tiles(lambda cut: rn[j, c, :, cut], wt_p.at[j], False)
        arrived(wt_f.at[j], plan["wt_fwd"] + j)
        for q in range(CHUNKS):
            arrived(fn.at[j, pl.ds(q * ct, ct), :], plan["fwd"] + j * CHUNKS + q)
        grad_tiles(lambda cut: fn[j, :, cut], wt_f.at[j], False)

    ones = jnp.ones((8, wout.shape[1]), jnp.bfloat16)
    nt = (((1,), (1,)), ((), ()))
    for i in range(dn // tile):
        cut = slice(i * tile, (i + 1) * tile)
        g = grad[cut, :]
        wout[cut, :] = g.astype(jnp.bfloat16)
        prod = g * wch[c, cut, :].astype(jnp.float32)
        hi = prod.astype(jnp.bfloat16)
        lo = (prod - hi.astype(jnp.float32)).astype(jnp.bfloat16)
        sums = lax.dot_general(ones, hi, nt, preferred_element_type=jnp.float32)
        sums += lax.dot_general(ones, lo, nt, preferred_element_type=jnp.float32)
        gcols = pl.ds(pl.multiple_of(f * dn + i * tile, LANES), tile)
        gg[f, :, cut] = sums / gain[:, gcols]
    for o in range(1, nf):
        send(gg.at[f], gg.at[f], plan["gain"] + o, plan["gain"] + nf - o, {"fsdp": lax.rem(f + o, nf)})
    l_wout = local(7, wout, wgrad_h.at[0])

    for j in range(1, chips):
        for q in range(CHUNKS):
            rows = pl.ds(q * ct, ct)
            arrived(kp.at[j, rows, :], plan["kp"] + j * CHUNKS + q)
        kacc[...] += kp[j].astype(jnp.float32)
    kout[...] = kacc[...].astype(jnp.bfloat16)
    l_kout = local(8, kout, keys_h.at[0])

    for k in range(2):
        arrived(og.at[2 * (1 - h) + k], plan["yag"] + k)
    l_og = [local(10 + g, og.at[g], outer_h.at[:, pl.ds(g * LANES, LANES)]) for g in range(4)]

    for o in range(1, nf):
        arrived(gg.at[lax.rem(f + o, nf)], plan["gain"] + o)
    for d in range(nf):
        gout[:, d * dn:(d + 1) * dn] = gg[d, 0:1, :]
    l_gout = local(9, gout, ggrad_h)

    for copy in sent:
        copy.wait_send()
    for copy in [l_wout, l_kout, l_gout] + l_og:
        copy.wait()


def exchange(nf, nr, token_ids, hidden, norm_gain, key_weight, key_cot, frag_base, frag_local):
    tok, d = hidden.shape[1:]
    dn, kw = frag_base.shape
    chips, outer = nf // CORES, nr // PAIR
    plan, n_sem = semaphore_plan(nf, nr)
    bf, f32 = jnp.bfloat16, jnp.float32
    vmem = pltpu.VMEM
    anyspace = pl.BlockSpec(memory_space=pl.ANY)
    scratch = [
        vmem((1, tok), jnp.int32), vmem((tok, d), bf), vmem((1, d), f32), vmem((CORES, dn, kw), bf),
        vmem((tok, kw), bf), vmem((dn, kw), f32), vmem((dn, kw), bf),
        vmem((nf, tok, dn), bf), vmem((chips, CORES, tok, dn), bf), vmem((tok, dn), bf),
        vmem((chips, tok, dn), bf),
        vmem((tok, kw), bf), vmem((tok, kw), bf), vmem((chips, tok, kw), bf), vmem((chips, tok, kw), bf),
        vmem((chips, tok, kw), bf), vmem((chips, tok, kw), bf), vmem((tok, kw), f32), vmem((tok, kw), bf),
        vmem((dn, kw), f32), vmem((dn, kw), bf), vmem((nf, 8, dn), f32), vmem((1, d), f32),
        vmem((4, dn, LANES), bf), vmem((2, dn, LANES), bf), vmem((2, dn, LANES), bf),
        vmem((2, outer, dn // outer, LANES), bf), vmem((4, dn, LANES), bf),
        pltpu.SemaphoreType.DMA((n_sem,)), pltpu.SemaphoreType.DMA((n_sem,)), pltpu.SemaphoreType.DMA((14,)),
    ]
    return pl.pallas_call(
        functools.partial(kernel, nf, nr, plan),
        out_shape=(
            jax.ShapeDtypeStruct((1, tok, kw), bf),
            jax.ShapeDtypeStruct((1, dn, kw), bf),
            jax.ShapeDtypeStruct((1, d), f32),
            jax.ShapeDtypeStruct((dn, kw), bf),
        ),
        in_specs=[anyspace] * 7,
        out_specs=(anyspace,) * 4,
        scratch_shapes=scratch,
        compiler_params=pltpu.CompilerParams(
            collective_id=0, has_side_effects=True, vmem_limit_bytes=56 * 1024 * 1024
        ),
    )(token_ids, hidden, norm_gain, key_weight, key_cot, frag_base, frag_local)


def body(nf, nr, token_ids, hidden, norm_gain, key_weight, key_cot, frag_base, frag_local, momentum):
    keys, weight_grad, gain_grad, total = exchange(
        nf, nr, token_ids, hidden, norm_gain, key_weight, key_cot, frag_base, frag_local
    )
    outer_grad = total.astype(jnp.float32) / nr
    momentum_next = nesterov_mu * momentum.astype(jnp.float32) + outer_grad
    new_params = frag_base - outer_rate * (nesterov_mu * momentum_next + outer_grad)
    return (keys, weight_grad, gain_grad, new_params, momentum_next.astype(jnp.bfloat16))


def solution(mesh):
    return jax.shard_map(
        functools.partial(body, mesh.shape["fsdp"], mesh.shape["rep"]),
        mesh=mesh,
        in_specs=(
            P("rep", "fsdp"),
            P("rep", "fsdp", None),
            P("rep", None),
            P("rep", "fsdp", None),
            P("rep", "fsdp", None),
            P("fsdp", None),
            P("rep", "fsdp", None),
            P("fsdp", None),
        ),
        out_specs=(
            P("rep", "fsdp", None),
            P("rep", "fsdp", None),
            P("rep", None),
            P("fsdp", None),
            P("fsdp", None),
        ),
        check_vma=False,
    )
```

time: 227 us -> 57.6 us (0.25)
  waiting for transfers between devices: 179 us -> 0 us
  Pallas kernels: 0 us -> 50.6 us
  between operations: 13.8 us -> 0.69 us
  matrix products: 11.1 us -> 0 us
  blocking collectives: 10.8 us -> 0 us
  other arithmetic: 11.3 us -> 3.64 us
    all_gather x2 -> x0, waiting for transfers between devices: 140 us -> none  [the longest x1 109 us: outer_step(): grads_all = lax.all_gather(pseudo_grad[None], 'rep', axis=0, tiled=True)]
    pallas_call x0 -> x1, Pallas kernels: none -> 50.6 us  [exchange(): pl.pallas_call(functools.partial(kernel, nf, nr, plan), out_shape=(jax.Sh...]
    reduce_scatter x1 -> x0, waiting for transfers between devices: 38.5 us -> none  [inner_step(): lax.psum_scatter(lax.dot_general(h_cols, weighted, (((0,), (0,)), ((), ()...]
    dot_general x3 -> x0, matrix products: 11.1 us -> none  [the longest x1 4.19 us: inner_step(): keys_acc = jnp.dot(h_cols, w_rows, preferred_element_type=jnp.float32)]
    psum x1 -> x0, blocking collectives: 10.8 us -> none  [inner_step(): gain_grad = lax.psum(gain_part, 'fsdp')]
    reduce_sum x3 -> x0, other arithmetic: 5.55 us -> none  [the longest x1 4.93 us: outer_step(): outer_grad = jnp.sum(grads_all.astype(jnp.float32), 0) / replicas]
    unnamed x12 -> x13, local copies, waits for them, and re-layouts: 0.02 us -> 2.3 us
    convert_element_type x3 -> x1, other arithmetic: 5.72 us -> 3.64 us  [body(): momentum_next.astype(jnp.bfloat16)]
  transfers between devices with their start and end apart: 3 -> 0, of which waited for: 3 -> 0; matrix products, arithmetic and copies ran while one was open for 10% -> 0% of each run, Pallas kernels for 0% -> 0%
where the time goes in v1:
time: 57.6 us; the launch traced here: 57.3 us
  Pallas kernels  50.6 us (88%)
  other arithmetic  3.64 us (6%)
  local copies, waits for them, and re-layouts  2.3 us (4%)
  between operations  0.69 us (1%)
    pallas_call x1, Pallas kernels, exchange(): pl.pallas_call(functools.partial(kernel, nf, nr, plan), out_shape=(jax.Sh...  50.6 us
    convert_element_type x1, other arithmetic, body(): momentum_next.astype(jnp.bfloat16)  3.64 us
    unnamed x13, local copies, waits for them, and re-layouts  2.3 us

profile of v1, /device:TPU:0, one launch (start us, length us, event | category | flops | bytes accessed | tf_op | source)
XLA Modules:
  0.0 57.3 jit_solution(9119660566674640587)
XLA Ops:
  0.6 0.0 copy-start
  0.6 0.0 copy-start.1
  0.7 50.6 %shard_map.119 = (bf16[1,256,512]{2,1,0:T(8,128)(2,1)}, bf16[1,1024,512]{2,1,0:T(8,128)(2,1)}, f32[1,4096]{1,0:T(1,128)}, bf16[1024,512]{1,0:T(8,128)(2,1)}) custom-call(s32[1,256]{1,0:T(1,128)} %ids_h.1, bf16[1,256,4096]{2,1,0:T(8,128)(2,1)} %hid_h.1, f32[1,4096]{1,0:T(1,128)} %gain_h.1, bf16[1,1024,512]{2,1,0:T(8,128)(2,1)} %w_h.1, ...), custom_call_target="tpu_custom_call" | custom-call | tf_op jit(solution)/shard_map/pallas_call | solution.py:341
  51.3 0.0 copy-done
  51.3 0.0 copy-done.1
  51.3 0.0 copy-start.3
  51.3 0.0 copy-start.2
  51.3 3.6 %fusion.1 = (bf16[1024,512]{1,0:T(8,128)(2,1)}, f32[1024,512]{1,0:T(8,128)}) fusion(bf16[1024,512]{1,0:T(8,128)(2,1)} %get-tuple-element.12, bf16[1024,512]{1,0:T(8,128)(2,1)S(1)} %copy-done.1, f32[1024,512]{1,0:T(8,128)S(1)} %copy-done), kind=kLoop, calls=%fused_computation.3 | loop fusion | flops 5242880 | bytes 7340032 | tf_op jit(solution)/shard_map/convert_element_type | solution.py:365
  55.0 0.0 copy-start.4
  55.0 0.0 copy-done.3
  55.0 0.7 %copy.16 = bf16[1,256,512]{2,1,0:T(8,128)(2,1)} copy(bf16[1,256,512]{2,1,0:T(8,128)(2,1)S(1)} %copy-done.3) | data formatting | bytes 524288
  55.7 0.0 copy-done.2
  55.7 1.0 %copy.17 = bf16[1,1024,512]{2,1,0:T(8,128)(2,1)} copy(bf16[1,1024,512]{2,1,0:T(8,128)(2,1)S(1)} %copy-done.2) | data formatting | bytes 2097152
  56.7 0.0 copy-done.4
  56.7 0.6 %copy.18 = f32[1,4096]{1,0:T(1,128)} copy(f32[1,4096]{1,0:T(1,128)S(1)} %copy-done.4) | data formatting | bytes 32768
Async XLA Ops:
  0.6 50.7 %copy-start = (f32[1024,512]{1,0:T(8,128)S(1)}, f32[1024,512]{1,0:T(8,128)}, u32[]{:S(2)}) copy-start(f32[1024,512]{1,0:T(8,128)} %base_h.1) | copy-start | bytes 6291460
  0.6 50.7 %copy-start.1 = (bf16[1024,512]{1,0:T(8,128)(2,1)S(1)}, bf16[1024,512]{1,0:T(8,128)(2,1)}, u32[]{:S(2)}) copy-start(bf16[1024,512]{1,0:T(8,128)(2,1)} %param.15) | copy-start | bytes 3145732
  51.3 3.7 %copy-start.3 = (bf16[1,256,512]{2,1,0:T(8,128)(2,1)S(1)}, bf16[1,256,512]{2,1,0:T(8,128)(2,1)}, u32[]{:S(2)}) copy-start(bf16[1,256,512]{2,1,0:T(8,128)(2,1)} %get-tuple-element.20) | copy-start | bytes 786436
  51.3 4.4 %copy-start.2 = (bf16[1,1024,512]{2,1,0:T(8,128)(2,1)S(1)}, bf16[1,1024,512]{2,1,0:T(8,128)(2,1)}, u32[]{:S(2)}) copy-start(bf16[1,1024,512]{2,1,0:T(8,128)(2,1)} %get-tuple-element.21) | copy-start | bytes 3145732
  55.0 1.7 %copy-start.4 = (f32[1,4096]{1,0:T(1,128)S(1)}, f32[1,4096]{1,0:T(1,128)}, u32[]{:S(2)}) copy-start(f32[1,4096]{1,0:T(1,128)} %get-tuple-element.22) | copy-start | bytes 49156

commit v2 on v1

--- a/solution.py
+++ b/solution.py
@@ -31,7 +31,7 @@
         return first
 
 
-def semaphore_plan(nf, nr):
+def semaphore_plan(nf, nr, pieces):
     chips, outer = nf // CORES, nr // PAIR
     c = Counter()
     plan = {
@@ -44,10 +44,10 @@
         "fwd": c.take(chips * CHUNKS),
         "kp": c.take(chips * CHUNKS),
         "gain": c.take(nf),
-        "y": c.take(2),
-        "z": c.take(2 * outer),
-        "zag": c.take(2 * outer),
-        "yag": c.take(2),
+        "y": c.take(pieces),
+        "z": c.take(pieces * outer),
+        "zag": c.take(pieces * outer),
+        "yag": c.take(pieces),
     }
     return plan, c.n
 
@@ -57,7 +57,7 @@
 
 
 def kernel(
-    nf, nr, plan,
+    nf, nr, pieces, plan,
     ids_h, hid_h, gain_h, w_h, cot_h, base_h, loc_h,
     keys_h, wgrad_h, ggrad_h, outer_h,
     ids, hid, gain, wch, cot, base, loc,
@@ -69,7 +69,10 @@
     tok = hid.shape[0]
     dn = base.shape[0]
     chips, outer = nf // CORES, nr // PAIR
-    zrows = dn // outer
+    width = base.shape[1] // PAIR
+    groups = width // LANES
+    prows = dn * groups // pieces
+    zrows = prows // outer
     ct = tok // CHUNKS
     f = lax.axis_index("fsdp")
     r = lax.axis_index("rep")
@@ -124,6 +127,29 @@
     def arrived(dst, rid):
         copy_of(dst, dst, rid, rid, {"fsdp": sib}).wait_recv()
 
+    def peer(j):
+        return {"fsdp": chip_at(j) * CORES + c}
+
+    step = min(64, prows)
+
+    def pseudo(half, k, rows):
+        g, b = k % groups, k // groups
+        cols = pl.ds(pl.multiple_of(half * width + g * LANES, LANES), LANES)
+        rows = pl.ds(pl.multiple_of(b * prows + rows * step, step), step)
+        return (base[rows, cols] - loc[rows, cols].astype(jnp.float32)).astype(jnp.bfloat16)
+
+    def pseudo_rows(k, i, carry):
+        ps[k, pl.ds(pl.multiple_of(i * step, step), step), :] = pseudo(1 - h, k, i)
+        return carry
+
+    l_base.wait()
+    l_loc.wait()
+    for k in range(pieces):
+        lax.fori_loop(0, prows // step, functools.partial(pseudo_rows, k), 0)
+        if k == 0:
+            pl.semaphore_wait(barrier, greeted)
+        send(ps.at[k], yr.at[k], plan["y"] + k, plan["y"] + k, {"rep": partner})
+
     l_ids.wait()
     row = lax.broadcasted_iota(jnp.int32, (tok, tok), 0)
     col = lax.broadcasted_iota(jnp.int32, (tok, tok), 1)
@@ -135,16 +161,6 @@
     l_cot.wait()
     wt[...] = (loss_weight * cot[...].astype(jnp.float32)).astype(jnp.bfloat16)
 
-    pl.semaphore_wait(barrier, greeted)
-
-    def peer(j):
-        return {"fsdp": chip_at(j) * CORES + c}
-
-    for j in range(1, chips):
-        send(wt, wt_p.at[chips - j], plan["wt"] + j, plan["wt"] + chips - j, peer(j))
-    send(wt, wt_s, plan["wt_sib"], plan["wt_sib"], {"fsdp": sib})
-    send(w_h.at[0], wch.at[c], plan["w"], plan["w"], {"fsdp": sib})
-
     l_gain.wait()
     l_hid.wait()
     sub = 16
@@ -159,6 +175,11 @@
         return carry
 
     for q in range(CHUNKS):
+        if q == 1:
+            send(w_h.at[0], wch.at[c], plan["w"], plan["w"], {"fsdp": sib})
+            for j in range(1, chips):
+                send(wt, wt_p.at[chips - j], plan["wt"] + j, plan["wt"] + chips - j, peer(j))
+            send(wt, wt_s, plan["wt_sib"], plan["wt_sib"], {"fsdp": sib})
         lax.fori_loop(q * (ct // sub), (q + 1) * (ct // sub), norm_rows, 0)
         rows = pl.ds(q * ct, ct)
         for j in range(1, chips):
@@ -171,26 +192,6 @@
             )
     send(nrm.at[sib], sn, plan["sib"], plan["sib"], {"fsdp": sib})
 
-    l_base.wait()
-    l_loc.wait()
-    step = 64
-
-    def pseudo_rows(i, carry):
-        rows = pl.ds(pl.multiple_of(i * step, step), step)
-        for g in range(4):
-            cols = slice(g * LANES, (g + 1) * LANES)
-            ps[g, rows, :] = (base[rows, cols] - loc[rows, cols].astype(jnp.float32)).astype(jnp.bfloat16)
-        return carry
-
-    lax.fori_loop(0, dn // step, pseudo_rows, 0)
-    for k in range(2):
-        send(ps.at[2 * (1 - h) + k], yr.at[k], plan["y"] + k, plan["y"] + k, {"rep": partner})
-
-    l_w.wait()
-    arrived(wch.at[1 - c], plan["w"])
-    kacc[...] = jnp.dot(nrm[2 * x], wch[0], preferred_element_type=jnp.float32)
-    kacc[...] += jnp.dot(nrm[2 * x + 1], wch[1], preferred_element_type=jnp.float32)
-
     tile = min(256, dn)
 
     def grad_tiles(rows_of, tokens_of, first):
@@ -202,18 +203,12 @@
             else:
                 grad[cut, :] += term
 
-    grad_tiles(lambda cut: nrm[f, :, cut], wt, True)
-    arrived(wt_s, plan["wt_sib"])
-    arrived(sn, plan["sib"])
-    grad_tiles(lambda cut: sn[:, cut], wt_s, False)
-
-    for j in range(1, chips):
-        arrived(wt_p.at[j], plan["wt"] + j)
-        send(wt_p.at[j], wt_f.at[j], plan["wt_fwd"] + j, plan["wt_fwd"] + j, {"fsdp": sib})
-
     def peer_chunk(q):
         rows = pl.ds(q * ct, ct)
         for j in range(1, chips):
+            if q == 0:
+                arrived(wt_p.at[j], plan["wt"] + j)
+                send(wt_p.at[j], wt_f.at[j], plan["wt_fwd"] + j, plan["wt_fwd"] + j, {"fsdp": sib})
             arrived(rn.at[j, :, rows, :], plan["nrm"] + j * CHUNKS + q)
             send(
                 rn.at[j, 1 - c, rows, :], fn.at[j, rows, :],
@@ -227,9 +222,22 @@
                 plan["kp"] + j * CHUNKS + q, plan["kp"] + (chips - j) * CHUNKS + q, peer(j),
             )
 
+    def own_keys(half):
+        n = tok // 2
+        rows = slice(half * n, (half + 1) * n)
+        kacc[rows, :] = jnp.dot(nrm[2 * x, rows, :], wch[0], preferred_element_type=jnp.float32)
+        kacc[rows, :] += jnp.dot(nrm[2 * x + 1, rows, :], wch[1], preferred_element_type=jnp.float32)
+
     def pair_sum(k):
         arrived(yr.at[k], plan["y"] + k)
-        ys[k] = (ps[2 * h + k].astype(jnp.float32) + yr[k].astype(jnp.float32)).astype(jnp.bfloat16)
+
+        def some(i, carry):
+            rows = pl.ds(pl.multiple_of(i * step, step), step)
+            total = pseudo(h, k, i).astype(jnp.float32) + yr[k, rows, :].astype(jnp.float32)
+            ys[k, rows, :] = total.astype(jnp.bfloat16)
+            return carry
+
+        lax.fori_loop(0, prows // step, some, 0)
         for o in range(1, outer):
             send(
                 ys.at[k, pl.ds(pl.multiple_of(z_at(o) * zrows, 16), zrows), :],
@@ -245,30 +253,56 @@
         for o in range(1, outer):
             arrived(zr.at[k, o], plan["z"] + k * outer + o)
             total += zr[k, o].astype(jnp.float32)
-        og[2 * h + k, mine, :] = total.astype(jnp.bfloat16)
+        og[h, k, mine, :] = total.astype(jnp.bfloat16)
         for o in range(1, outer):
             send(
-                og.at[2 * h + k, mine, :], og.at[2 * h + k, mine, :],
+                og.at[h, k, mine, :], og.at[h, k, mine, :],
                 plan["zag"] + k * outer + o, plan["zag"] + k * outer + outer - o,
                 {"rep": z_at(o) * PAIR + h},
             )
 
+    def outer_out(half, k):
+        g, b = k % groups, k // groups
+        cols = pl.ds(pl.multiple_of(half * width + g * LANES, LANES), LANES)
+        return og.at[half, k], outer_h.at[pl.ds(b * prows, prows), cols]
+
+    l_og = []
+
     def outer_back(k):
         for o in range(1, outer):
             there = pl.ds(pl.multiple_of(z_at(o) * zrows, 16), zrows)
-            arrived(og.at[2 * h + k, there, :], plan["zag"] + k * outer + o)
-        send(og.at[2 * h + k], og.at[2 * h + k], plan["yag"] + k, plan["yag"] + k, {"rep": partner})
-
+            arrived(og.at[h, k, there, :], plan["zag"] + k * outer + o)
+        send(og.at[h, k], og.at[h, k], plan["yag"] + k, plan["yag"] + k, {"rep": partner})
+        l_og.append(local(10 + k, *outer_out(h, k)))
+
+    def if_piece(step_of, k):
+        if k < pieces:
+            step_of(k)
+
+    pair_sum(0)
+    pair_sum(1)
+    l_w.wait()
+    arrived(wch.at[1 - c], plan["w"])
+    own_keys(0)
+    if_piece(pair_sum, 2)
+    outer_sum(0)
+    if_piece(pair_sum, 3)
+    outer_sum(1)
     peer_chunk(0)
-    pair_sum(0)
+    outer_back(0)
+    if_piece(outer_sum, 2)
+    own_keys(1)
+    outer_back(1)
+    if_piece(outer_sum, 3)
     peer_chunk(1)
-    pair_sum(1)
-    outer_sum(0)
+    if_piece(outer_back, 2)
+    grad_tiles(lambda cut: nrm[f, :, cut], wt, True)
+    if_piece(outer_back, 3)
     peer_chunk(2)
-    outer_sum(1)
-    outer_back(0)
+    arrived(wt_s, plan["wt_sib"])
+    arrived(sn, plan["sib"])
+    grad_tiles(lambda cut: sn[:, cut], wt_s, False)
     peer_chunk(3)
-    outer_back(1)
 
     for j in range(1, chips):
         grad_tiles(lambda cut: rn[j, c, :, cut], wt_p.at[j], False)
@@ -302,9 +336,9 @@
     kout[...] = kacc[...].astype(jnp.bfloat16)
     l_kout = local(8, kout, keys_h.at[0])
 
-    for k in range(2):
-        arrived(og.at[2 * (1 - h) + k], plan["yag"] + k)
-    l_og = [local(10 + g, og.at[g], outer_h.at[:, pl.ds(g * LANES, LANES)]) for g in range(4)]
+    for k in range(pieces):
+        arrived(og.at[1 - h, k], plan["yag"] + k)
+        l_og.append(local(10 + pieces + k, *outer_out(1 - h, k)))
 
     for o in range(1, nf):
         arrived(gg.at[lax.rem(f + o, nf)], plan["gain"] + o)
@@ -322,7 +356,9 @@
     tok, d = hidden.shape[1:]
     dn, kw = frag_base.shape
     chips, outer = nf // CORES, nr // PAIR
-    plan, n_sem = semaphore_plan(nf, nr)
+    pieces = 4 if dn // 2 // outer % 16 == 0 else 2
+    prows = dn * (kw // PAIR // LANES) // pieces
+    plan, n_sem = semaphore_plan(nf, nr, pieces)
     bf, f32 = jnp.bfloat16, jnp.float32
     vmem = pltpu.VMEM
     anyspace = pl.BlockSpec(memory_space=pl.ANY)
@@ -334,12 +370,12 @@
         vmem((tok, kw), bf), vmem((tok, kw), bf), vmem((chips, tok, kw), bf), vmem((chips, tok, kw), bf),
         vmem((chips, tok, kw), bf), vmem((chips, tok, kw), bf), vmem((tok, kw), f32), vmem((tok, kw), bf),
         vmem((dn, kw), f32), vmem((dn, kw), bf), vmem((nf, 8, dn), f32), vmem((1, d), f32),
-        vmem((4, dn, LANES), bf), vmem((2, dn, LANES), bf), vmem((2, dn, LANES), bf),
-        vmem((2, outer, dn // outer, LANES), bf), vmem((4, dn, LANES), bf),
-        pltpu.SemaphoreType.DMA((n_sem,)), pltpu.SemaphoreType.DMA((n_sem,)), pltpu.SemaphoreType.DMA((14,)),
+        vmem((pieces, prows, LANES), bf), vmem((pieces, prows, LANES), bf), vmem((pieces, prows, LANES), bf),
+        vmem((pieces, outer, prows // outer, LANES), bf), vmem((PAIR, pieces, prows, LANES), bf),
+        pltpu.SemaphoreType.DMA((n_sem,)), pltpu.SemaphoreType.DMA((n_sem,)), pltpu.SemaphoreType.DMA((10 + 2 * pieces,)),
     ]
     return pl.pallas_call(
-        functools.partial(kernel, nf, nr, plan),
+        functools.partial(kernel, nf, nr, pieces, plan),
         out_shape=(
             jax.ShapeDtypeStruct((1, tok, kw), bf),
             jax.ShapeDtypeStruct((1, dn, kw), bf),

time: 57.6 us -> 51.8 us (0.90)
  Pallas kernels: 50.6 us -> 45 us
    pallas_call x1, Pallas kernels: 50.6 us -> 45 us  [exchange(): pl.pallas_call(functools.partial(kernel, nf, nr, pieces, plan), out_shape...]
where the time goes in v2:
time: 51.8 us; the launch traced here: 51.6 us
  Pallas kernels  45 us (87%)
  other arithmetic  3.64 us (7%)
  local copies, waits for them, and re-layouts  2.3 us (4%)
  between operations  0.69 us (1%)
    pallas_call x1, Pallas kernels, exchange(): pl.pallas_call(functools.partial(kernel, nf, nr, pieces, plan), out_shape...  45 us
    convert_element_type x1, other arithmetic, body(): momentum_next.astype(jnp.bfloat16)  3.64 us
    unnamed x13, local copies, waits for them, and re-layouts  2.3 us

profile of v2, /device:TPU:0, one launch (start us, length us, event | category | flops | bytes accessed | tf_op | source)
XLA Modules:
  0.0 51.6 jit_solution(15347212788486589522)
XLA Ops:
  0.6 0.0 copy-start
  0.6 0.0 copy-start.1
  0.7 45.0 %shard_map.119 = (bf16[1,256,512]{2,1,0:T(8,128)(2,1)}, bf16[1,1024,512]{2,1,0:T(8,128)(2,1)}, f32[1,4096]{1,0:T(1,128)}, bf16[1024,512]{1,0:T(8,128)(2,1)}) custom-call(s32[1,256]{1,0:T(1,128)} %ids_h.1, bf16[1,256,4096]{2,1,0:T(8,128)(2,1)} %hid_h.1, f32[1,4096]{1,0:T(1,128)} %gain_h.1, bf16[1,1024,512]{2,1,0:T(8,128)(2,1)} %w_h.1, ...), custom_call_target="tpu_custom_call" | custom-call | tf_op jit(solution)/shard_map/pallas_call | solution.py:377
  45.6 0.0 copy-done
  45.6 0.0 copy-done.1
  45.7 0.0 copy-start.3
  45.7 0.0 copy-start.2
  45.7 3.6 %fusion.1 = (bf16[1024,512]{1,0:T(8,128)(2,1)}, f32[1024,512]{1,0:T(8,128)}) fusion(bf16[1024,512]{1,0:T(8,128)(2,1)} %get-tuple-element.12, bf16[1024,512]{1,0:T(8,128)(2,1)S(1)} %copy-done.1, f32[1024,512]{1,0:T(8,128)S(1)} %copy-done), kind=kLoop, calls=%fused_computation.3 | loop fusion | flops 5242880 | bytes 7340032 | tf_op jit(solution)/shard_map/convert_element_type | solution.py:401
  49.3 0.0 copy-start.4
  49.3 0.0 copy-done.3
  49.3 0.7 %copy.16 = bf16[1,256,512]{2,1,0:T(8,128)(2,1)} copy(bf16[1,256,512]{2,1,0:T(8,128)(2,1)S(1)} %copy-done.3) | data formatting | bytes 524288
  50.0 0.0 copy-done.2
  50.0 1.0 %copy.17 = bf16[1,1024,512]{2,1,0:T(8,128)(2,1)} copy(bf16[1,1024,512]{2,1,0:T(8,128)(2,1)S(1)} %copy-done.2) | data formatting | bytes 2097152
  51.0 0.0 copy-done.4
  51.0 0.6 %copy.18 = f32[1,4096]{1,0:T(1,128)} copy(f32[1,4096]{1,0:T(1,128)S(1)} %copy-done.4) | data formatting | bytes 32768
Async XLA Ops:
  0.6 45.0 %copy-start = (f32[1024,512]{1,0:T(8,128)S(1)}, f32[1024,512]{1,0:T(8,128)}, u32[]{:S(2)}) copy-start(f32[1024,512]{1,0:T(8,128)} %base_h.1) | copy-start | bytes 6291460
  0.6 45.0 %copy-start.1 = (bf16[1024,512]{1,0:T(8,128)(2,1)S(1)}, bf16[1024,512]{1,0:T(8,128)(2,1)}, u32[]{:S(2)}) copy-start(bf16[1024,512]{1,0:T(8,128)(2,1)} %param.15) | copy-start | bytes 3145732
  45.7 3.7 %copy-start.3 = (bf16[1,256,512]{2,1,0:T(8,128)(2,1)S(1)}, bf16[1,256,512]{2,1,0:T(8,128)(2,1)}, u32[]{:S(2)}) copy-start(bf16[1,256,512]{2,1,0:T(8,128)(2,1)} %get-tuple-element.20) | copy-start | bytes 786436
  45.7 4.4 %copy-start.2 = (bf16[1,1024,512]{2,1,0:T(8,128)(2,1)S(1)}, bf16[1,1024,512]{2,1,0:T(8,128)(2,1)}, u32[]{:S(2)}) copy-start(bf16[1,1024,512]{2,1,0:T(8,128)(2,1)} %get-tuple-element.21) | copy-start | bytes 3145732
  49.3 1.7 %copy-start.4 = (f32[1,4096]{1,0:T(1,128)S(1)}, f32[1,4096]{1,0:T(1,128)}, u32[]{:S(2)}) copy-start(f32[1,4096]{1,0:T(1,128)} %get-tuple-element.22) | copy-start | bytes 49156

commit v3 on v2

--- a/solution.py
+++ b/solution.py
@@ -73,7 +73,10 @@
     groups = width // LANES
     prows = dn * groups // pieces
     zrows = prows // outer
-    ct = tok // CHUNKS
+    unit = tok // 16
+    edges = [0, 4 * unit, 9 * unit, 14 * unit, tok]
+    spans = [pl.ds(a, b - a) for a, b in zip(edges[:-1], edges[1:])]
+    early, late = slice(0, edges[2]), slice(edges[2], tok)
     f = lax.axis_index("fsdp")
     r = lax.axis_index("rep")
     x, c = lax.div(f, CORES), lax.rem(f, CORES)
@@ -92,13 +95,16 @@
         copy.start()
         return copy
 
-    l_cot = local(0, cot_h.at[0], cot)
-    l_ids = local(1, ids_h, ids)
     l_gain = local(2, gain_h, gain)
-    l_hid = local(3, hid_h.at[0], hid)
+    l_hid = []
+    for q, rows in enumerate(spans):
+        l_hid.append(local(10 + 4 * pieces + q, hid_h.at[0, rows, :], hid.at[rows, :]))
+        if q == 0:
+            l_base = local(5, base_h, base)
+            l_loc = local(6, loc_h.at[0], loc)
+            l_ids = local(1, ids_h, ids)
+            l_cot = local(0, cot_h.at[0], cot)
     l_w = local(4, w_h.at[0], wch.at[c])
-    l_base = local(5, base_h, base)
-    l_loc = local(6, loc_h.at[0], loc)
 
     barrier = pltpu.get_barrier_semaphore()
     greeted = 0
@@ -130,6 +136,35 @@
     def peer(j):
         return {"fsdp": chip_at(j) * CORES + c}
 
+    l_gain.wait()
+    sub = 16
+
+    def norm_rows(i, carry):
+        rows = pl.ds(pl.multiple_of(i * sub, sub), sub)
+        v = hid[rows, :].astype(jnp.float32)
+        inv = lax.rsqrt(jnp.mean(v * v, -1, keepdims=True) + norm_eps)
+        for d in range(nf):
+            part = hid[rows, d * dn:(d + 1) * dn].astype(jnp.float32)
+            nrm[d, rows, :] = (part * inv * gain[:, d * dn:(d + 1) * dn]).astype(jnp.bfloat16)
+        return carry
+
+    def norm_chunk(q):
+        l_hid[q].wait()
+        lax.fori_loop(edges[q] // sub, edges[q + 1] // sub, norm_rows, 0)
+        if q == 0:
+            pl.semaphore_wait(barrier, greeted)
+        rows = spans[q]
+        for j in range(1, chips):
+            send(
+                nrm.at[pl.ds(chip_at(j) * CORES, CORES), rows, :],
+                rn.at[chips - j, :, rows, :],
+                plan["nrm"] + j * CHUNKS + q,
+                plan["nrm"] + (chips - j) * CHUNKS + q,
+                peer(j),
+            )
+
+    norm_chunk(0)
+
     step = min(64, prows)
 
     def pseudo(half, k, rows):
@@ -146,9 +181,10 @@
     l_loc.wait()
     for k in range(pieces):
         lax.fori_loop(0, prows // step, functools.partial(pseudo_rows, k), 0)
-        if k == 0:
-            pl.semaphore_wait(barrier, greeted)
         send(ps.at[k], yr.at[k], plan["y"] + k, plan["y"] + k, {"rep": partner})
+
+    norm_chunk(1)
+    send(w_h.at[0], wch.at[c], plan["w"], plan["w"], {"fsdp": sib})
 
     l_ids.wait()
     row = lax.broadcasted_iota(jnp.int32, (tok, tok), 0)
@@ -161,52 +197,25 @@
     l_cot.wait()
     wt[...] = (loss_weight * cot[...].astype(jnp.float32)).astype(jnp.bfloat16)
 
-    l_gain.wait()
-    l_hid.wait()
-    sub = 16
-
-    def norm_rows(i, carry):
-        rows = pl.ds(pl.multiple_of(i * sub, sub), sub)
-        v = hid[rows, :].astype(jnp.float32)
-        inv = lax.rsqrt(jnp.mean(v * v, -1, keepdims=True) + norm_eps)
-        for d in range(nf):
-            part = hid[rows, d * dn:(d + 1) * dn].astype(jnp.float32)
-            nrm[d, rows, :] = (part * inv * gain[:, d * dn:(d + 1) * dn]).astype(jnp.bfloat16)
-        return carry
-
-    for q in range(CHUNKS):
-        if q == 1:
-            send(w_h.at[0], wch.at[c], plan["w"], plan["w"], {"fsdp": sib})
-            for j in range(1, chips):
-                send(wt, wt_p.at[chips - j], plan["wt"] + j, plan["wt"] + chips - j, peer(j))
-            send(wt, wt_s, plan["wt_sib"], plan["wt_sib"], {"fsdp": sib})
-        lax.fori_loop(q * (ct // sub), (q + 1) * (ct // sub), norm_rows, 0)
-        rows = pl.ds(q * ct, ct)
-        for j in range(1, chips):
-            send(
-                nrm.at[pl.ds(chip_at(j) * CORES, CORES), rows, :],
-                rn.at[chips - j, :, rows, :],
-                plan["nrm"] + j * CHUNKS + q,
-                plan["nrm"] + (chips - j) * CHUNKS + q,
-                peer(j),
-            )
-    send(nrm.at[sib], sn, plan["sib"], plan["sib"], {"fsdp": sib})
+    for j in range(1, chips):
+        send(wt, wt_p.at[chips - j], plan["wt"] + j, plan["wt"] + chips - j, peer(j))
+    send(wt, wt_s, plan["wt_sib"], plan["wt_sib"], {"fsdp": sib})
 
     tile = min(256, dn)
 
-    def grad_tiles(rows_of, tokens_of, first):
+    def grad_tiles(rows_of, weighted, first):
         for i in range(dn // tile):
             cut = slice(i * tile, (i + 1) * tile)
-            term = transposed_dot(rows_of(cut), tokens_of[...])
+            term = transposed_dot(rows_of(cut), weighted())
             if first:
                 grad[cut, :] = term
             else:
                 grad[cut, :] += term
 
     def peer_chunk(q):
-        rows = pl.ds(q * ct, ct)
+        rows = spans[q]
         for j in range(1, chips):
-            if q == 0:
+            if q == 1:
                 arrived(wt_p.at[j], plan["wt"] + j)
                 send(wt_p.at[j], wt_f.at[j], plan["wt_fwd"] + j, plan["wt_fwd"] + j, {"fsdp": sib})
             arrived(rn.at[j, :, rows, :], plan["nrm"] + j * CHUNKS + q)
@@ -261,11 +270,6 @@
                 {"rep": z_at(o) * PAIR + h},
             )
 
-    def outer_out(half, k):
-        g, b = k % groups, k // groups
-        cols = pl.ds(pl.multiple_of(half * width + g * LANES, LANES), LANES)
-        return og.at[half, k], outer_h.at[pl.ds(b * prows, prows), cols]
-
     l_og = []
 
     def outer_back(k):
@@ -273,49 +277,67 @@
             there = pl.ds(pl.multiple_of(z_at(o) * zrows, 16), zrows)
             arrived(og.at[h, k, there, :], plan["zag"] + k * outer + o)
         send(og.at[h, k], og.at[h, k], plan["yag"] + k, plan["yag"] + k, {"rep": partner})
-        l_og.append(local(10 + k, *outer_out(h, k)))
-
-    def if_piece(step_of, k):
+
+    def outer_out(half, k, slot):
+        g, b = k % groups, k // groups
+        cols = pl.ds(pl.multiple_of(half * width + g * LANES, LANES), LANES)
+        l_og.append(local(10 + slot, og.at[half, k], outer_h.at[pl.ds(b * prows, prows), cols]))
+
+    def pair_back(k):
+        arrived(og.at[1 - h, k], plan["yag"] + k)
+        outer_out(1 - h, k, pieces + k)
+
+    def piece(step_of, k):
         if k < pieces:
             step_of(k)
 
     pair_sum(0)
+    norm_chunk(2)
     pair_sum(1)
+    norm_chunk(3)
+    send(nrm.at[sib], sn, plan["sib"], plan["sib"], {"fsdp": sib})
+    outer_sum(0)
+    piece(pair_sum, 2)
+    outer_sum(1)
+    piece(pair_sum, 3)
     l_w.wait()
     arrived(wch.at[1 - c], plan["w"])
-    own_keys(0)
-    if_piece(pair_sum, 2)
-    outer_sum(0)
-    if_piece(pair_sum, 3)
-    outer_sum(1)
     peer_chunk(0)
     outer_back(0)
-    if_piece(outer_sum, 2)
+    piece(outer_sum, 2)
+    own_keys(0)
+    outer_back(1)
+    piece(outer_sum, 3)
     own_keys(1)
-    outer_back(1)
-    if_piece(outer_sum, 3)
     peer_chunk(1)
-    if_piece(outer_back, 2)
-    grad_tiles(lambda cut: nrm[f, :, cut], wt, True)
-    if_piece(outer_back, 3)
-    peer_chunk(2)
+    piece(outer_back, 2)
+    grad_tiles(lambda cut: nrm[f, :, cut], lambda: wt[...], True)
+    piece(outer_back, 3)
+    for k in range(pieces):
+        outer_out(h, k, k)
     arrived(wt_s, plan["wt_sib"])
     arrived(sn, plan["sib"])
-    grad_tiles(lambda cut: sn[:, cut], wt_s, False)
+    grad_tiles(lambda cut: sn[:, cut], lambda: wt_s[...], False)
+    for j in range(1, chips):
+        grad_tiles(lambda cut: rn[j, c, early, cut], lambda: wt_p[j, early, :], False)
+        arrived(wt_f.at[j], plan["wt_fwd"] + j)
+        for q in range(2):
+            arrived(fn.at[j, spans[q], :], plan["fwd"] + j * CHUNKS + q)
+        grad_tiles(lambda cut: fn[j, early, cut], lambda: wt_f[j, early, :], False)
+    peer_chunk(2)
     peer_chunk(3)
 
     for j in range(1, chips):
-        grad_tiles(lambda cut: rn[j, c, :, cut], wt_p.at[j], False)
-        arrived(wt_f.at[j], plan["wt_fwd"] + j)
-        for q in range(CHUNKS):
-            arrived(fn.at[j, pl.ds(q * ct, ct), :], plan["fwd"] + j * CHUNKS + q)
-        grad_tiles(lambda cut: fn[j, :, cut], wt_f.at[j], False)
-
+        for q in range(2, CHUNKS):
+            arrived(fn.at[j, spans[q], :], plan["fwd"] + j * CHUNKS + q)
     ones = jnp.ones((8, wout.shape[1]), jnp.bfloat16)
     nt = (((1,), (1,)), ((), ()))
     for i in range(dn // tile):
         cut = slice(i * tile, (i + 1) * tile)
         g = grad[cut, :]
+        for j in range(1, chips):
+            g += transposed_dot(rn[j, c, late, cut], wt_p[j, late, :])
+            g += transposed_dot(fn[j, late, cut], wt_f[j, late, :])
         wout[cut, :] = g.astype(jnp.bfloat16)
         prod = g * wch[c, cut, :].astype(jnp.float32)
         hi = prod.astype(jnp.bfloat16)
@@ -330,15 +352,14 @@
 
     for j in range(1, chips):
         for q in range(CHUNKS):
-            rows = pl.ds(q * ct, ct)
+            rows = spans[q]
             arrived(kp.at[j, rows, :], plan["kp"] + j * CHUNKS + q)
         kacc[...] += kp[j].astype(jnp.float32)
     kout[...] = kacc[...].astype(jnp.bfloat16)
     l_kout = local(8, kout, keys_h.at[0])
 
     for k in range(pieces):
-        arrived(og.at[1 - h, k], plan["yag"] + k)
-        l_og.append(local(10 + pieces + k, *outer_out(1 - h, k)))
+        pair_back(k)
 
     for o in range(1, nf):
         arrived(gg.at[lax.rem(f + o, nf)], plan["gain"] + o)
@@ -372,7 +393,7 @@
         vmem((dn, kw), f32), vmem((dn, kw), bf), vmem((nf, 8, dn), f32), vmem((1, d), f32),
         vmem((pieces, prows, LANES), bf), vmem((pieces, prows, LANES), bf), vmem((pieces, prows, LANES), bf),
         vmem((pieces, outer, prows // outer, LANES), bf), vmem((PAIR, pieces, prows, LANES), bf),
-        pltpu.SemaphoreType.DMA((n_sem,)), pltpu.SemaphoreType.DMA((n_sem,)), pltpu.SemaphoreType.DMA((10 + 2 * pieces,)),
+        pltpu.SemaphoreType.DMA((n_sem,)), pltpu.SemaphoreType.DMA((n_sem,)), pltpu.SemaphoreType.DMA((10 + 4 * pieces + CHUNKS,)),
     ]
     return pl.pallas_call(
         functools.partial(kernel, nf, nr, pieces, plan),

time: 51.8 us -> 51.5 us (level)
  no operation moved by 1% of the time
where the time goes in v3:
time: 51.5 us; the launch traced here: 51.3 us
  Pallas kernels  44.7 us (87%)
  other arithmetic  3.64 us (7%)
  local copies, waits for them, and re-layouts  2.3 us (4%)
  between operations  0.69 us (1%)
    pallas_call x1, Pallas kernels, exchange(): pl.pallas_call(functools.partial(kernel, nf, nr, pieces, plan), out_shape...  44.7 us
    convert_element_type x1, other arithmetic, body(): momentum_next.astype(jnp.bfloat16)  3.64 us
    unnamed x13, local copies, waits for them, and re-layouts  2.3 us

profile of v3, /device:TPU:0, one launch (start us, length us, event | category | flops | bytes accessed | tf_op | source)
XLA Modules:
  0.0 51.3 jit_solution(8197736330724551131)
XLA Ops:
  0.6 0.0 copy-start
  0.6 0.0 copy-start.1
  0.7 44.7 %shard_map.119 = (bf16[1,256,512]{2,1,0:T(8,128)(2,1)}, bf16[1,1024,512]{2,1,0:T(8,128)(2,1)}, f32[1,4096]{1,0:T(1,128)}, bf16[1024,512]{1,0:T(8,128)(2,1)}) custom-call(s32[1,256]{1,0:T(1,128)} %ids_h.1, bf16[1,256,4096]{2,1,0:T(8,128)(2,1)} %hid_h.1, f32[1,4096]{1,0:T(1,128)} %gain_h.1, bf16[1,1024,512]{2,1,0:T(8,128)(2,1)} %w_h.1, ...), custom_call_target="tpu_custom_call" | custom-call | tf_op jit(solution)/shard_map/pallas_call | solution.py:398
  45.3 0.0 copy-done
  45.3 0.0 copy-done.1
  45.4 0.0 copy-start.3
  45.4 0.0 copy-start.2
  45.4 3.6 %fusion.1 = (bf16[1024,512]{1,0:T(8,128)(2,1)}, f32[1024,512]{1,0:T(8,128)}) fusion(bf16[1024,512]{1,0:T(8,128)(2,1)} %get-tuple-element.12, bf16[1024,512]{1,0:T(8,128)(2,1)S(1)} %copy-done.1, f32[1024,512]{1,0:T(8,128)S(1)} %copy-done), kind=kLoop, calls=%fused_computation.3 | loop fusion | flops 5242880 | bytes 7340032 | tf_op jit(solution)/shard_map/convert_element_type | solution.py:422
  49.0 0.0 copy-start.4
  49.0 0.0 copy-done.3
  49.0 0.7 %copy.16 = bf16[1,256,512]{2,1,0:T(8,128)(2,1)} copy(bf16[1,256,512]{2,1,0:T(8,128)(2,1)S(1)} %copy-done.3) | data formatting | bytes 524288
  49.7 0.0 copy-done.2
  49.7 1.0 %copy.17 = bf16[1,1024,512]{2,1,0:T(8,128)(2,1)} copy(bf16[1,1024,512]{2,1,0:T(8,128)(2,1)S(1)} %copy-done.2) | data formatting | bytes 2097152
  50.7 0.0 copy-done.4
  50.7 0.6 %copy.18 = f32[1,4096]{1,0:T(1,128)} copy(f32[1,4096]{1,0:T(1,128)S(1)} %copy-done.4) | data formatting | bytes 32768
Async XLA Ops:
  0.6 44.7 %copy-start = (f32[1024,512]{1,0:T(8,128)S(1)}, f32[1024,512]{1,0:T(8,128)}, u32[]{:S(2)}) copy-start(f32[1024,512]{1,0:T(8,128)} %base_h.1) | copy-start | bytes 6291460
  0.6 44.7 %copy-start.1 = (bf16[1024,512]{1,0:T(8,128)(2,1)S(1)}, bf16[1024,512]{1,0:T(8,128)(2,1)}, u32[]{:S(2)}) copy-start(bf16[1024,512]{1,0:T(8,128)(2,1)} %param.15) | copy-start | bytes 3145732
  45.4 3.7 %copy-start.3 = (bf16[1,256,512]{2,1,0:T(8,128)(2,1)S(1)}, bf16[1,256,512]{2,1,0:T(8,128)(2,1)}, u32[]{:S(2)}) copy-start(bf16[1,256,512]{2,1,0:T(8,128)(2,1)} %get-tuple-element.20) | copy-start | bytes 786436
  45.4 4.4 %copy-start.2 = (bf16[1,1024,512]{2,1,0:T(8,128)(2,1)S(1)}, bf16[1,1024,512]{2,1,0:T(8,128)(2,1)}, u32[]{:S(2)}) copy-start(bf16[1,1024,512]{2,1,0:T(8,128)(2,1)} %get-tuple-element.21) | copy-start | bytes 3145732
  49.0 1.7 %copy-start.4 = (f32[1,4096]{1,0:T(1,128)S(1)}, f32[1,4096]{1,0:T(1,128)}, u32[]{:S(2)}) copy-start(f32[1,4096]{1,0:T(1,128)} %get-tuple-element.22) | copy-start | bytes 49156
